TPU v7x, 32 devices: a whole 2x2x4 slice. The times are simulated.
32 devices in a mesh: dp: 16 (over z, y, x), tensor: 2 (over core).
Axes of the slice: x: 2, y: 2, z: 4, core: 2. Of those that a mesh axis runs over, the one named last changes fastest.
Arguments:
- tokens: bfloat16 [32768, 768], P(('dp', 'tensor')), may hold values from -6 to 6
- segment: int32 [32768], P('dp'), may hold values from -1 to 4, as said below
- ln1_gain: float32 [768], replicated, may hold values from 0.5 to 1.5
- w_qkv: bfloat16 [768, 3, 768], P(None, None, 'tensor'), may hold values from -0.21875 to 0.21875
- q_gain: float32 [64], replicated, may hold values from 0.25 to 1.75
- k_gain: float32 [64], replicated, may hold values from 0.25 to 1.75
- w_out: bfloat16 [768, 768], P('tensor'), may hold values from -1.75 to 1.75
- ln2_gain: float32 [768], replicated, may hold values from 0.5 to 1.5
- w_up: bfloat16 [768, 3072], P(None, 'tensor'), may hold values from -0.21875 to 0.21875
- w_down: bfloat16 [3072, 768], P('tensor'), may hold values from -0.109375 to 0.109375
- cotangent: bfloat16 [32768, 768], P(('dp', 'tensor')), may hold values from -6 to 6
Outputs:
- layer_out: bfloat16 [32768, 768], P(('dp', 'tensor'))
- input_grad: bfloat16 [32768, 768], P(('dp', 'tensor'))
- ln1_gain_grad: float32 [768], replicated
- qkv_grad: float32 [768, 3, 768], P('dp', None, 'tensor')
- q_gain_grad: float32 [64], replicated
- k_gain_grad: float32 [64], replicated
- proj_grad: float32 [768, 768], P('tensor', 'dp')
- ln2_gain_grad: float32 [768], replicated
- up_grad: float32 [768, 3072], P('dp', 'tensor')
- down_grad: float32 [3072, 768], P('tensor', 'dp')
Inputs may be any that keep to these rules, and one draw needn't show every extreme that they name: `segment`: rows k * 1024 to (k + 1) * 1024 - 1 form a sequence that holds 5 images of 196 positions, numbered 0 to 4 in order, and one run of 44 padding positions marked -1 before, between or after them.
All inputs are finite; a program needn't handle non-finite values.
Results may differ from a plain program's by a relative error of at most 0.017.
Values may be sent and summed in bfloat16 or wider, within the bound.
A program may use at most 192 MiB of HBM per device.

v0:
```python
import jax
import jax.numpy as jnp
from jax import lax
from jax.sharding import PartitionSpec as P

D = 768
HD = 64
LENGTH = 1024


epsilon = 1e-06
root_half = 0.7071067811865476
inv_root_two_pi = 0.3989422804014327


def contract(left, right, left_axis, right_axis):
    return lax.dot_general(
        left, right, (((left_axis,), (right_axis,)), ((), ())), preferred_element_type=jnp.float32
    )


def layer_norm(values, gain):
    centred = values - jnp.mean(values, axis=-1, keepdims=True)
    inverse = lax.rsqrt(jnp.mean(centred * centred, axis=-1, keepdims=True) + epsilon)
    standard = centred * inverse
    return (standard * gain, standard, inverse)


def norm_back(grad_normed, standard, inverse, gain):
    scaled = grad_normed * gain
    centred_grad = (
        scaled
        - jnp.mean(scaled, axis=-1, keepdims=True)
        - standard * jnp.mean(scaled * standard, axis=-1, keepdims=True)
    )
    return (centred_grad * inverse, grad_normed * standard)


def gelu_exact(values):
    return 0.5 * values * (1.0 + lax.erf(values * root_half))


def gelu_slope(values):
    return (
        0.5 * (1.0 + lax.erf(values * root_half))
        + values * jnp.exp(-0.5 * values * values) * inv_root_two_pi
    )


def gather_normed(values):
    return lax.all_gather(values, "tensor", axis=0, tiled=True)


def gather_middle(values):
    return lax.all_gather(values, "tensor", axis=0, tiled=True)


def sum_branch(term, row_count):
    return lax.psum_scatter(
        term(jnp.int32(0), row_count * lax.axis_size("tensor")),
        "tensor",
        scatter_dimension=0,
        tiled=True,
    )


def sum_feedfwd(term, row_count):
    return lax.psum_scatter(
        term(jnp.int32(0), row_count * lax.axis_size("tensor")).astype(jnp.bfloat16),
        "tensor",
        scatter_dimension=0,
        tiled=True,
    ).astype(jnp.float32)


def gather_cotangent(values):
    return lax.all_gather(values, "tensor", axis=0, tiled=True)


def gather_branch(values):
    return lax.all_gather(values, "tensor", axis=0, tiled=True)


def sum_middle_grad(term, row_count):
    return lax.psum_scatter(
        term(jnp.int32(0), row_count * lax.axis_size("tensor")).astype(jnp.bfloat16),
        "tensor",
        scatter_dimension=0,
        tiled=True,
    ).astype(jnp.float32)


def sum_input_grad(term, row_count):
    return lax.psum_scatter(
        term(jnp.int32(0), row_count * lax.axis_size("tensor")).astype(jnp.bfloat16),
        "tensor",
        scatter_dimension=0,
        tiled=True,
    ).astype(jnp.float32)


def row_product(source, weight, left_axis, right_axis):

    def term(offset, number):
        return contract(source, weight, left_axis, right_axis)

    return term


def block_scores(queries, key_rows, segment, offset, anchor, block_rows, scaling):
    query_block = lax.dynamic_slice_in_dim(queries, offset, block_rows, 0)
    key_block = lax.dynamic_slice_in_dim(key_rows, anchor, LENGTH, 0)
    scores = (
        jnp.einsum("qhd,khd->hqk", query_block, key_block, preferred_element_type=jnp.float32)
        * scaling
    )
    query_ids = lax.dynamic_slice_in_dim(segment, offset, block_rows, 0)
    key_ids = lax.dynamic_slice_in_dim(segment, anchor, LENGTH, 0)
    matching = query_ids[:, None] == key_ids[None, :]
    return (jnp.where(matching[None], scores, -1e30), query_block, key_block)


def attend(queries, key_rows, value_rows, segment):
    row_count, head_count, head_width = queries.shape
    block_rows = min(512, LENGTH)
    scaling = head_width ** (-0.5)

    def one_block(block_index):
        offset = block_index * block_rows
        anchor = offset // LENGTH * LENGTH
        scores, query_block, key_block = block_scores(
            queries, key_rows, segment, offset, anchor, block_rows, scaling
        )
        value_block = lax.dynamic_slice_in_dim(value_rows, anchor, LENGTH, 0)
        row_top = jnp.max(scores, axis=-1, keepdims=True)
        exponent = jnp.exp(scores - row_top)
        row_total = jnp.sum(exponent, axis=-1, keepdims=True)
        attn_probs = (exponent / row_total).astype(jnp.bfloat16)
        attended = jnp.einsum(
            "hqk,khd->qhd", attn_probs, value_block, preferred_element_type=jnp.float32
        )
        return (attended, (row_top + jnp.log(row_total))[:, :, 0])

    attended, log_totals = lax.map(one_block, jnp.arange(row_count // block_rows))
    return (attended.reshape(row_count, head_count * head_width), log_totals)


def attend_back(queries, key_rows, value_rows, segment, log_totals, grad_attended):
    row_count, head_count, head_width = queries.shape
    block_rows = min(512, LENGTH)
    scaling = head_width ** (-0.5)

    def one_block(carry, items):
        grad_keys, grad_values = carry
        block_index, log_block = items
        offset = block_index * block_rows
        anchor = offset // LENGTH * LENGTH
        scores, query_block, key_block = block_scores(
            queries, key_rows, segment, offset, anchor, block_rows, scaling
        )
        value_block = lax.dynamic_slice_in_dim(value_rows, anchor, LENGTH, 0)
        grad_block = lax.dynamic_slice_in_dim(grad_attended, offset, block_rows, 0)
        attn_probs = jnp.exp(scores - log_block[:, :, None])
        grad_probs = jnp.einsum(
            "qhd,khd->hqk", grad_block, value_block, preferred_element_type=jnp.float32
        )
        centre = jnp.sum(attn_probs * grad_probs, axis=-1, keepdims=True)
        grad_scores = (attn_probs * (grad_probs - centre)).astype(jnp.bfloat16)
        grad_query = (
            jnp.einsum("hqk,khd->qhd", grad_scores, key_block, preferred_element_type=jnp.float32)
            * scaling
        )
        key_terms = (
            jnp.einsum("hqk,qhd->khd", grad_scores, query_block, preferred_element_type=jnp.float32)
            * scaling
        )
        value_terms = jnp.einsum(
            "hqk,qhd->khd",
            attn_probs.astype(jnp.bfloat16),
            grad_block,
            preferred_element_type=jnp.float32,
        )
        grad_keys = lax.dynamic_update_slice_in_dim(
            grad_keys, lax.dynamic_slice_in_dim(grad_keys, anchor, LENGTH, 0) + key_terms, anchor, 0
        )
        grad_values = lax.dynamic_update_slice_in_dim(
            grad_values,
            lax.dynamic_slice_in_dim(grad_values, anchor, LENGTH, 0) + value_terms,
            anchor,
            0,
        )
        return ((grad_keys, grad_values), grad_query)

    zeros = jnp.zeros((row_count, head_count, head_width), jnp.float32)
    block_count = row_count // block_rows
    (grad_keys, grad_values), grad_queries = lax.scan(
        one_block, (zeros, zeros), (jnp.arange(block_count), log_totals)
    )
    return (grad_queries.reshape(row_count, head_count, head_width), grad_keys, grad_values)


def forward(tokens, segment, ln1_gain, w_qkv, q_gain, k_gain, w_out, ln2_gain, w_up, w_down, hooks):
    inputs = tokens.astype(jnp.float32)
    own_rows = tokens.shape[0]
    normed, standard_in, inverse_in = layer_norm(inputs, ln1_gain)
    normed_in = hooks[0](normed.astype(jnp.bfloat16))
    row_count = normed_in.shape[0]
    local_width = w_qkv.shape[2]
    head_count = local_width // HD
    projected = jnp.dot(
        normed_in, w_qkv.reshape(D, 3 * local_width), preferred_element_type=jnp.float32
    ).reshape(row_count, 3, head_count, HD)
    query_normed, query_standard, query_inverse = layer_norm(projected[:, 0], q_gain)
    key_normed, key_standard, key_inverse = layer_norm(projected[:, 1], k_gain)
    queries = query_normed.astype(jnp.bfloat16)
    key_rows = key_normed.astype(jnp.bfloat16)
    value_rows = projected[:, 2].astype(jnp.bfloat16)
    attended, log_totals = attend(queries, key_rows, value_rows, segment)
    attended = attended.astype(jnp.bfloat16)
    middle = inputs + hooks[2](row_product(attended, w_out, 1, 0), own_rows)
    normed, standard_mid, inverse_mid = layer_norm(middle, ln2_gain)
    normed_mid = hooks[1](normed.astype(jnp.bfloat16))
    hidden = jnp.dot(normed_mid, w_up, preferred_element_type=jnp.float32)
    activated = gelu_exact(hidden).astype(jnp.bfloat16)
    layer_out = middle + hooks[3](row_product(activated, w_down, 1, 0), own_rows)
    saved = (
        standard_in,
        inverse_in,
        normed_in,
        query_standard,
        query_inverse,
        key_standard,
        key_inverse,
        queries,
        key_rows,
        value_rows,
        log_totals,
        attended,
        standard_mid,
        inverse_mid,
        normed_mid,
        hidden,
        activated,
    )
    return (layer_out, saved)


def local(
    tokens, segment, ln1_gain, w_qkv, q_gain, k_gain, w_out, ln2_gain, w_up, w_down, cotangent
):
    own_rows = tokens.shape[0]
    hooks = (
        gather_normed,
        gather_middle,
        sum_branch,
        sum_feedfwd,
        gather_cotangent,
        gather_branch,
        sum_middle_grad,
        sum_input_grad,
    )
    layer_out, saved = forward(
        tokens, segment, ln1_gain, w_qkv, q_gain, k_gain, w_out, ln2_gain, w_up, w_down, hooks
    )
    saved = forward(
        tokens, segment, ln1_gain, w_qkv, q_gain, k_gain, w_out, ln2_gain, w_up, w_down, hooks
    )[1]
    (
        standard_in,
        inverse_in,
        normed_in,
        query_standard,
        query_inverse,
        key_standard,
        key_inverse,
        queries,
        key_rows,
        value_rows,
        log_totals,
        attended,
        standard_mid,
        inverse_mid,
        normed_mid,
        hidden,
        activated,
    ) = saved
    grad_rows = cotangent.astype(jnp.float32)
    grad_all = hooks[4](cotangent)
    grad_activated = contract(grad_all, w_down, 1, 1)
    down_grad = contract(activated, grad_all, 0, 0)
    grad_hidden = (grad_activated * gelu_slope(hidden)).astype(jnp.bfloat16)
    up_grad = contract(normed_mid, grad_hidden, 0, 0)
    grad_normed = hooks[6](row_product(grad_hidden, w_up, 1, 1), own_rows)
    grad_back, ln2_terms = norm_back(grad_normed, standard_mid, inverse_mid, ln2_gain)
    grad_middle = grad_rows + grad_back
    grad_branch = hooks[5](grad_middle.astype(jnp.bfloat16))
    proj_grad = contract(attended, grad_branch, 0, 0)
    grad_attended = contract(grad_branch, w_out, 1, 1).astype(jnp.bfloat16)
    row_count, local_width = grad_attended.shape
    grad_queries, grad_keys, grad_values = attend_back(
        queries,
        key_rows,
        value_rows,
        segment,
        log_totals,
        grad_attended.reshape(row_count, local_width // HD, HD),
    )
    grad_query_in, q_terms = norm_back(grad_queries, query_standard, query_inverse, q_gain)
    grad_key_in, k_terms = norm_back(grad_keys, key_standard, key_inverse, k_gain)
    grad_projected = (
        jnp.stack([grad_query_in, grad_key_in, grad_values], axis=1)
        .reshape(row_count, 3 * local_width)
        .astype(jnp.bfloat16)
    )
    qkv_grad = contract(normed_in, grad_projected, 0, 0).reshape(D, 3, local_width)
    grad_input = hooks[7](
        row_product(grad_projected, w_qkv.reshape(D, 3 * local_width), 1, 1), own_rows
    )
    grad_first, ln1_terms = norm_back(grad_input, standard_in, inverse_in, ln1_gain)
    input_grad = (grad_middle + grad_first).astype(jnp.bfloat16)
    weight_grads = (qkv_grad, proj_grad, up_grad, down_grad)
    qkv_grad, proj_grad, up_grad, down_grad = (
        lax.psum_scatter(weight_grads[0], "dp", scatter_dimension=0, tiled=True),
        lax.psum_scatter(weight_grads[1], "dp", scatter_dimension=1, tiled=True),
        lax.psum_scatter(weight_grads[2], "dp", scatter_dimension=0, tiled=True),
        lax.psum_scatter(weight_grads[3], "dp", scatter_dimension=1, tiled=True),
    )
    gain_terms = (
        jnp.sum(ln1_terms, axis=0),
        jnp.sum(q_terms, axis=(0, 1)),
        jnp.sum(k_terms, axis=(0, 1)),
        jnp.sum(ln2_terms, axis=0),
    )
    ln1_gain_grad, q_gain_grad, k_gain_grad, ln2_gain_grad = lax.psum(
        (gain_terms[0], gain_terms[1], gain_terms[2], gain_terms[3]), ("dp", "tensor")
    )
    return (
        layer_out.astype(jnp.bfloat16),
        input_grad,
        ln1_gain_grad,
        qkv_grad,
        q_gain_grad,
        k_gain_grad,
        proj_grad,
        ln2_gain_grad,
        up_grad,
        down_grad,
    )


def solution(mesh):
    return jax.shard_map(
        local,
        mesh=mesh,
        in_specs=(
            P(("dp", "tensor"), None),
            P("dp"),
            P(),
            P(None, None, "tensor"),
            P(),
            P(),
            P("tensor", None),
            P(),
            P(None, "tensor"),
            P("tensor", None),
            P(("dp", "tensor"), None),
        ),
        out_specs=(
            P(("dp", "tensor"), None),
            P(("dp", "tensor"), None),
            P(),
            P("dp", None, "tensor"),
            P(),
            P(),
            P("tensor", "dp"),
            P(),
            P("dp", "tensor"),
            P("tensor", "dp"),
        ),
        check_vma=False,
    )
```

profile of v0, /device:TPU:0, one launch (start us, length us, event | category | flops | bytes accessed | tf_op | source)
XLA Modules:
  0.0 1151.4 jit_solution(7275079989137587276)
XLA Ops:
  19.8 8.6 all-gather.6.cloned.1.call-done
  43.1 137.2 %while.45 = (s32[]{:T(128)}, bf16[4,512,6,64]{1,3,2,0:T(8,128)(2,1)}, s32[4]{0:T(128)S(1)}, bf16[2048,6,64]{0,2,1:T(8,128)(2,1)}, s32[2048]{0:T(1024)S(1)}, /*in...) while((s32[]{:T(128)}, bf16[4,512,6,64]{1,3,2,0:T(8,128)(2,1)}, ...), condition=%wide.region_9.10_spmd.clone, body=%wide.region_6.9_spmd.sunk.clone | while | flops 830997504 | bytes 73054656 | solution.py:144
  52.6 17.1 %fusion.182 = (f32[6,512]{1,0:T(8,128)S(1)}, f32[6,512,1024]{2,1,0:T(8,128)}) fusion(f32[6,512,1024]{2,1,0:T(8,128)} %fusion.181, pred[512,1024]{1,0:T(8,128)(4,1)S(1)} %broadcast_compare_fusion.9), kind=kOutput, calls=%fused_computation.173.clone.1.clone | output fusion | flops 18875392 | bytes 25702400 | tf_op jit(solution)/shard_map/while/body/eval_jaxpr/sub | solution.py:136
  86.9 17.1 %fusion.182 = (f32[6,512]{1,0:T(8,128)S(1)}, f32[6,512,1024]{2,1,0:T(8,128)}) fusion(f32[6,512,1024]{2,1,0:T(8,128)} %fusion.181, pred[512,1024]{1,0:T(8,128)(4,1)S(1)} %broadcast_compare_fusion.9), kind=kOutput, calls=%fused_computation.173.clone.1.clone | output fusion | flops 18875392 | bytes 25702400 | tf_op jit(solution)/shard_map/while/body/eval_jaxpr/sub | solution.py:136
  121.1 17.1 %fusion.182 = (f32[6,512]{1,0:T(8,128)S(1)}, f32[6,512,1024]{2,1,0:T(8,128)}) fusion(f32[6,512,1024]{2,1,0:T(8,128)} %fusion.181, pred[512,1024]{1,0:T(8,128)(4,1)S(1)} %broadcast_compare_fusion.9), kind=kOutput, calls=%fused_computation.173.clone.1.clone | output fusion | flops 18875392 | bytes 25702400 | tf_op jit(solution)/shard_map/while/body/eval_jaxpr/sub | solution.py:136
  155.4 17.1 %fusion.182 = (f32[6,512]{1,0:T(8,128)S(1)}, f32[6,512,1024]{2,1,0:T(8,128)}) fusion(f32[6,512,1024]{2,1,0:T(8,128)} %fusion.181, pred[512,1024]{1,0:T(8,128)(4,1)S(1)} %broadcast_compare_fusion.9), kind=kOutput, calls=%fused_computation.173.clone.1.clone | output fusion | flops 18875392 | bytes 25702400 | tf_op jit(solution)/shard_map/while/body/eval_jaxpr/sub | solution.py:136
  188.8 56.7 %while.46 = (s32[]{:T(128)}, bf16[4,512,6,64]{1,3,2,0:T(8,128)(2,1)}, f32[4,6,512]{2,1,0:T(8,128)S(1)}, s32[4]{0:T(128)S(1)}, bf16[2048,6,64]{0,2,1:T(8,128)(2,1...) while((s32[]{:T(128)}, ...), condition=%wide.region_17.18_spmd.clone, body=%wide.region_14.17_spmd.sunk.clone | while | flops 843576320 | bytes 61610440 | solution.py:144
  254.3 15.8 %reduce-scatter.14.cloned.1.call-done = f32[1024,768]{1,0:T(8,128)} async-done(((f32[2048,768]{1,0:T(8,128)}), f32[1024,768]{1,0:T(8,128)}) %reduce-scatter.14.cloned.1.call-update) | async-done | bytes 3145744 | tf_op jit(solution)/shard_map/reduce_scatter | solution.py:59
  278.8 12.8 %all-gather.12.cloned.1.call-done = bf16[2048,768]{1,0:T(8,128)(2,1)} async-done(((bf16[1024,768]{1,0:T(8,128)(2,1)}), bf16[2048,768]{1,0:T(8,128)(2,1)}) %all-gather.12.cloned.1.call-update) | async-done | bytes 3145744 | tf_op jit(solution)/shard_map/all_gather | solution.py:55
  291.6 10.3 fusion.105
  306.3 11.1 fusion.60
  326.5 12.2 %reduce-scatter.16.cloned.1.call-done = bf16[1024,768]{1,0:T(8,128)(2,1)} async-done(((bf16[2048,768]{1,0:T(8,128)(2,1)}), bf16[1024,768]{1,0:T(8,128)(2,1)}) %reduce-scatter.16.cloned.1.call-update) | async-done | bytes 1572880 | tf_op jit(solution)/shard_map/reduce_scatter | solution.py:85
  369.2 127.5 %while.47 = (s32[]{:T(128)}, f32[2048,6,64]{0,2,1:T(8,128)}, f32[2048,6,64]{0,2,1:T(8,128)}, f32[4,512,6,64]{1,3,2,0:T(8,128)}, s32[4]{0:T(128)S(1)}, /*index=5*...) while((s32[]{:T(128)}, f32[2048,6,64]{0,2,1:T(8,128)}, ...), condition=%wide.region_26.27_spmd.clone, body=%wide.region_24.26_spmd.sunk.clone | while | flops 2062349312 | bytes 151632432 | solution.py:196
  530.0 11.6 %reduce-scatter.18.cloned.1.call-done = bf16[1024,768]{1,0:T(8,128)(2,1)} async-done(((bf16[2048,768]{1,0:T(8,128)(2,1)}), bf16[1024,768]{1,0:T(8,128)(2,1)}) %reduce-scatter.18.cloned.1.call-update) | async-done | bytes 1572880 | tf_op jit(solution)/shard_map/reduce_scatter | solution.py:94
  552.0 13.4 %all-gather.8.cloned.1.call-done = bf16[2048,768]{1,0:T(8,128)(2,1)} async-done(((bf16[1024,768]{1,0:T(8,128)(2,1)}), bf16[2048,768]{1,0:T(8,128)(2,1)}) %all-gather.8.cloned.1.call-update) | async-done | bytes 3145744 | tf_op jit(solution)/shard_map/all_gather | solution.py:55
  565.4 13.7 %convolution_convert_fusion.2 = bf16[2048,768]{1,0:T(8,128)(2,1)} fusion(bf16[1536,768]{1,0:T(8,128)(2,1)} %param.26, bf16[2048,768]{1,0:T(8,128)(2,1)} %all-gather.8.cloned.1.call-done, bf16[768,1536]{1,0:T(8,128)(2,1)S(1)} %copy-done), kind=kOutput, calls=%fused_computation.102 | convolution fusion | flops 9680977920 | bytes 11010048 | tf_op jit(solution)/shard_map/dot_general | solution.py:17
  579.2 12.1 %fusion.61 = f32[1536,768]{0,1:T(8,128)} fusion(bf16[2048,768]{1,0:T(8,128)(2,1)} %all-gather.10.cloned.1.call-done, f32[2048,1536]{1,0:T(8,128)} %fusion.105), kind=kOutput, calls=%fused_computation.80 | convolution fusion | flops 4847566848 | bytes 20447232 | tf_op jit(solution)/shard_map/dot_general | solution.py:17
  591.3 9.7 fusion.107
  606.5 8.6 fusion.88
  615.8 41.4 %all-reduce = (f32[768]{0:T(1024)}, f32[64]{0:T(128)}, f32[64]{0:T(128)}, f32[768]{0:T(1024)}) all-reduce(f32[768]{0:T(1024)S(1)} %get-tuple-element.359, f32[64]{0:T(128)S(1)} %get-tuple-element.355, f32[64]{0:T(128)S(1)} %get-tuple-element.349, f32[768]{0:T(1024)S(1)} %copy-done.46), channel_id=1, replica_groups=mesh['dp'=16,'tensor'=2] {'dp','tensor'}, use_global_device_ids=true, to_apply=%region_35.36 | all-reduce | flops 1664 | bytes 13312 | tf_op jit(solution)/shard_map/psum | solution.py:334
  661.6 74.4 %reduce-scatter.26.cloned.1.call-done = f32[1536,48]{0,1:T(8,128)} async-done(((f32[1536,768]{0,1:T(8,128)}), f32[1536,48]{0,1:T(8,128)}) %reduce-scatter.26.cloned.1.call-update) | async-done | bytes 294928 | tf_op jit(solution)/shard_map/reduce_scatter | solution.py:326
  736.0 141.0 %reduce-scatter.24.cloned.1.call-done = f32[48,1536]{1,0:T(8,128)} async-done(((f32[768,1536]{1,0:T(8,128)}), f32[48,1536]{1,0:T(8,128)}) %reduce-scatter.24.cloned.1.call-update) | async-done | bytes 294928 | tf_op jit(solution)/shard_map/reduce_scatter | solution.py:325
  877.0 128.9 %reduce-scatter.22.cloned.1.call-done = f32[384,48]{0,1:T(8,128)} async-done(((f32[384,768]{0,1:T(8,128)}), f32[384,48]{0,1:T(8,128)}) %reduce-scatter.22.cloned.1.call-update) | async-done | bytes 73744 | tf_op jit(solution)/shard_map/reduce_scatter | solution.py:324
  1006.0 138.7 %reduce-scatter.20.cloned.1.call-done = f32[48,3,384]{2,0,1:T(8,128)} async-done(((f32[768,3,384]{2,0,1:T(8,128)}), f32[48,3,384]{2,0,1:T(8,128)}) %reduce-scatter.20.cloned.1.call-update) | async-done | bytes 221200 | tf_op jit(solution)/shard_map/reduce_scatter | solution.py:323
  (365 shorter events, 394.8 us)
Async XLA Ops:
  7.2 284.4 %copy-start = (bf16[768,1536]{1,0:T(8,128)(2,1)S(1)}, bf16[768,1536]{1,0:T(8,128)(2,1)}, u32[]{:S(2)}) copy-start(bf16[768,1536]{1,0:T(8,128)(2,1)} %param.25) | copy-start | bytes 7077892
  7.2 21.2 %all-gather.6.cloned.1.call-start = ((), (), s32[]{:S(2)}) async-start(), calls=%async_computation.9 | async-start | bytes 4718592 | tf_op jit(solution)/shard_map/all_gather | solution.py:51
  13.4 240.8 %reduce-scatter.10.cloned.1.call-start = ((), (), s32[]{:S(2)}) async-start(), calls=%async_computation.10 | async-start | bytes 9437184 | tf_op jit(solution)/shard_map/reduce_scatter | solution.py:59
  52.6 17.1 %copy-start.12 = (bf16[2048,6,64]{0,2,1:T(8,128)(2,1)S(1)}, bf16[2048,6,64]{0,2,1:T(8,128)(2,1)}, u32[]{:S(2)}) copy-start(bf16[2048,6,64]{0,2,1:T(8,128)(2,1)} %get-tuple-element.750) | copy-start | bytes 4718596 | tf_op jit(solution)/shard_map/while
  52.6 17.1 %copy-start.21 = (bf16[4,512,6,64]{1,3,2,0:T(8,128)(2,1)S(1)}, bf16[4,512,6,64]{1,3,2,0:T(8,128)(2,1)}, u32[]{:S(2)}) copy-start(bf16[4,512,6,64]{1,3,2,0:T(8,128)(2,1)} %get-tuple-element.740) | copy-start | bytes 4718596 | tf_op jit(solution)/shard_map/while
  86.9 17.1 %copy-start.12 = (bf16[2048,6,64]{0,2,1:T(8,128)(2,1)S(1)}, bf16[2048,6,64]{0,2,1:T(8,128)(2,1)}, u32[]{:S(2)}) copy-start(bf16[2048,6,64]{0,2,1:T(8,128)(2,1)} %get-tuple-element.750) | copy-start | bytes 4718596 | tf_op jit(solution)/shard_map/while
  86.9 17.1 %copy-start.21 = (bf16[4,512,6,64]{1,3,2,0:T(8,128)(2,1)S(1)}, bf16[4,512,6,64]{1,3,2,0:T(8,128)(2,1)}, u32[]{:S(2)}) copy-start(bf16[4,512,6,64]{1,3,2,0:T(8,128)(2,1)} %get-tuple-element.740) | copy-start | bytes 4718596 | tf_op jit(solution)/shard_map/while
  121.1 17.1 %copy-start.12 = (bf16[2048,6,64]{0,2,1:T(8,128)(2,1)S(1)}, bf16[2048,6,64]{0,2,1:T(8,128)(2,1)}, u32[]{:S(2)}) copy-start(bf16[2048,6,64]{0,2,1:T(8,128)(2,1)} %get-tuple-element.750) | copy-start | bytes 4718596 | tf_op jit(solution)/shard_map/while
  121.1 17.1 %copy-start.21 = (bf16[4,512,6,64]{1,3,2,0:T(8,128)(2,1)S(1)}, bf16[4,512,6,64]{1,3,2,0:T(8,128)(2,1)}, u32[]{:S(2)}) copy-start(bf16[4,512,6,64]{1,3,2,0:T(8,128)(2,1)} %get-tuple-element.740) | copy-start | bytes 4718596 | tf_op jit(solution)/shard_map/while
  155.4 17.1 %copy-start.12 = (bf16[2048,6,64]{0,2,1:T(8,128)(2,1)S(1)}, bf16[2048,6,64]{0,2,1:T(8,128)(2,1)}, u32[]{:S(2)}) copy-start(bf16[2048,6,64]{0,2,1:T(8,128)(2,1)} %get-tuple-element.750) | copy-start | bytes 4718596 | tf_op jit(solution)/shard_map/while
  155.4 17.1 %copy-start.21 = (bf16[4,512,6,64]{1,3,2,0:T(8,128)(2,1)S(1)}, bf16[4,512,6,64]{1,3,2,0:T(8,128)(2,1)}, u32[]{:S(2)}) copy-start(bf16[4,512,6,64]{1,3,2,0:T(8,128)(2,1)} %get-tuple-element.740) | copy-start | bytes 4718596 | tf_op jit(solution)/shard_map/while
  188.0 82.1 %reduce-scatter.14.cloned.1.call-start = ((), (), s32[]{:S(2)}) async-start(), calls=%async_computation.14 | async-start | bytes 9437184 | tf_op jit(solution)/shard_map/reduce_scatter | solution.py:59
  254.2 37.3 %all-gather.12.cloned.1.call-start = ((), (), s32[]{:S(2)}) async-start(), calls=%async_computation.15 | async-start | bytes 4718592 | tf_op jit(solution)/shard_map/all_gather | solution.py:55
  278.1 28.1 %all-gather.10.cloned.1.call-start = ((), (), s32[]{:S(2)}) async-start(), calls=%async_computation.13 | async-start | bytes 4718592 | tf_op jit(solution)/shard_map/all_gather | solution.py:77
  278.7 60.0 %reduce-scatter.16.cloned.1.call-start = ((), (), s32[]{:S(2)}) async-start(), calls=%async_computation.16 | async-start | bytes 4718592 | tf_op jit(solution)/shard_map/reduce_scatter | solution.py:85
  326.5 34.3 %all-gather.14.cloned.1.call-start = ((), (), s32[]{:S(2)}) async-start(), calls=%async_computation.17 | async-start | bytes 4718592 | tf_op jit(solution)/shard_map/all_gather | solution.py:81
  347.3 194.2 %reduce-scatter.18.cloned.1.call-start = ((), (), s32[]{:S(2)}) async-start(), calls=%async_computation.18 | async-start | bytes 4718592 | tf_op jit(solution)/shard_map/reduce_scatter | solution.py:94
  529.3 36.1 %all-gather.8.cloned.1.call-start = ((), (), s32[]{:S(2)}) async-start(), calls=%async_computation.11 | async-start | bytes 4718592 | tf_op jit(solution)/shard_map/all_gather | solution.py:55
  530.0 16.9 %copy-start.41 = (f32[768]{0:T(1024)S(1)}, f32[768]{0:T(1024)}, u32[]{:S(2)}) copy-start(f32[768]{0:T(1024)} %param.24) | copy-start | bytes 9220
  552.0 105.2 %reduce-scatter.12.cloned.1.call-start = ((), (), s32[]{:S(2)}) async-start(), calls=%async_computation.12 | async-start | bytes 4718592 | tf_op jit(solution)/shard_map/reduce_scatter | solution.py:68
  579.1 156.9 %reduce-scatter.26.cloned.1.call-start = ((), (), s32[]{:S(2)}) async-start(), calls=%async_computation.22 | async-start | bytes 5013504 | tf_op jit(solution)/shard_map/reduce_scatter | solution.py:326
  591.3 285.8 %reduce-scatter.24.cloned.1.call-start = ((), (), s32[]{:S(2)}) async-start(), calls=%async_computation.21 | async-start | bytes 5013504 | tf_op jit(solution)/shard_map/reduce_scatter | solution.py:325
  601.0 404.9 %reduce-scatter.22.cloned.1.call-start = ((), (), s32[]{:S(2)}) async-start(), calls=%async_computation.20 | async-start | bytes 1253376 | tf_op jit(solution)/shard_map/reduce_scatter | solution.py:324
  606.5 538.2 %reduce-scatter.20.cloned.1.call-start = ((), (), s32[]{:S(2)}) async-start(), calls=%async_computation.19 | async-start | bytes 3760128 | tf_op jit(solution)/shard_map/reduce_scatter | solution.py:323
  (76 other events, 295.8 us)
Sparse Core Ops, SparseCore 0:
  13.6 14.8 all-gather.5
  188.1 15.6 reduce-scatter.9
  254.3 15.6 reduce-scatter.13
  278.2 13.2 all-gather.11
  292.9 13.2 all-gather.9
  326.6 12.0 reduce-scatter.15
  347.4 13.2 all-gather.13
  529.4 12.0 reduce-scatter.17
  552.1 13.2 all-gather.7
  579.3 12.0 reduce-scatter.11
  597.9 138.0 reduce-scatter.25
  741.6 135.3 reduce-scatter.23
  883.1 122.8 reduce-scatter.21
  1012.3 132.3 reduce-scatter.19
where the time goes:
time: 1160 us; the launch traced here: 1150 us
  waiting for transfers between devices  570 us (49%)
  matrix products  276 us (24%)
  other arithmetic  170 us (15%)
  local copies, waits for them, and re-layouts  68.6 us (6%)
  blocking collectives  41.4 us (4%)
  between operations  14.7 us (1%)
    reduce_scatter x1, waiting for transfers between devices, local(): lax.psum_scatter(weight_grads[2], 'dp', scatter_dimension=0, tiled=True)  141 us
    reduce_scatter x1, waiting for transfers between devices, local(): lax.psum_scatter(weight_grads[0], 'dp', scatter_dimension=0, tiled=True)  139 us
    reduce_scatter x1, waiting for transfers between devices, local(): lax.psum_scatter(weight_grads[1], 'dp', scatter_dimension=1, tiled=True)  129 us
    dot_general x11, matrix products, contract(): lax.dot_general(left, right, (((left_axis,), (right_axis,)), ((), ())), p...  86 us
    reduce_scatter x1, waiting for transfers between devices, local(): lax.psum_scatter(weight_grads[3], 'dp', scatter_dimension=1, tiled=True)  74.4 us
    sub x4, other arithmetic, one_block(): exponent = jnp.exp(scores - row_top)  68.2 us
    dot_general x12, matrix products, block_scores(): jnp.einsum('qhd,khd->hqk', query_block, key_block, preferred_element_type...  57.9 us
    dot_general x8, matrix products, one_block(): jnp.einsum('hqk,khd->qhd', attn_probs, value_block, preferred_element_typ...  42.5 us
  transfers between devices with their start and end apart: 14, of which 12 were waited for; matrix products, arithmetic and copies ran while one was open for 10% of the time, Pallas kernels for 0%

commit v1 on v0

v1 whole, which is shorter than its diff:
```python
import functools

import jax
import jax.numpy as jnp
from jax import lax
from jax.experimental import pallas as pl
from jax.experimental.pallas import tpu as pltpu
from jax.sharding import PartitionSpec as P

D = 768
HD = 64
LENGTH = 1024
PATCHES = 196
IMAGES = 5
PADDING = LENGTH - IMAGES * PATCHES
PADDED = 1040
PAIRS = 6
EPS = 1e-06
MESH = pl.DeviceIdType.MESH
f32, bf16 = jnp.float32, jnp.bfloat16

WINDOWS = [
    (PATCHES * i // 16 * 16, 208, PATCHES * i, PATCHES * (i + 1)) for i in range(IMAGES)
] + [(976, 48, 980, 1024)]

FF_CHUNKS = 6
FW = 256
CHUNKS = 10
BITS = 4


def dot(left, right):
    return jnp.dot(left, right, preferred_element_type=f32)


def dot_nt(left, right):
    return lax.dot_general(left, right, (((1,), (1,)), ((), ())), preferred_element_type=f32)


def dot_tn(left, right):
    return lax.dot_general(left, right, (((0,), (0,)), ((), ())), preferred_element_type=f32)


def gelu_and_slope(h):
    e = jnp.exp(h * h * -0.5)
    t = 1.0 / (1.0 + jnp.abs(h) * (0.3275911 * 0.7071067811865476))
    poly = t * (
        0.5 * 0.254829592
        + t
        * (
            0.5 * -0.284496736
            + t * (0.5 * 1.421413741 + t * (0.5 * -1.453152027 + t * (0.5 * 1.061405429)))
        )
    )
    tail = poly * e
    phi = jnp.where(h >= 0, 1.0 - tail, tail)
    return h * phi, phi + h * e * 0.3989422804014327


def split(x):
    high = x.astype(bf16)
    return high, (x - high.astype(f32)).astype(bf16)


def iota(shape, axis):
    return lax.broadcasted_iota(jnp.int32, shape, axis)


def norm_rows(x):
    centred = x - jnp.mean(x, axis=-1, keepdims=True)
    inverse = lax.rsqrt(jnp.mean(centred * centred, axis=-1, keepdims=True) + EPS)
    return centred * inverse, inverse


def norm_rows_back(grad, standard, inverse, gain):
    c = grad * gain
    return inverse * (
        c
        - jnp.mean(c, axis=-1, keepdims=True)
        - standard * jnp.mean(c * standard, axis=-1, keepdims=True)
    )


def swap(pos):
    return (pos & 4) | (pos & 1) | ((pos & 8) >> 2) | ((pos & 2) << 2)


def kernel(
    dp_low,
    slot_ref,
    tok,
    cot,
    ln1,
    ln2,
    qgain,
    kgain,
    wqkv,
    wout,
    wup,
    wdn,
    lay_out,
    inp_out,
    up_out,
    dn_out,
    pr_out,
    qk_out,
    gains_out,
    wup_x,
    wdn_x,
    tokv,
    cotv,
    xp,
    cp,
    ni,
    q,
    k,
    v,
    invq,
    invk,
    lse,
    nlg,
    dlt,
    mid,
    outa,
    gna,
    big,
    wus,
    wds,
    wq,
    wo,
    do,
    sbuf,
    r0,
    af,
    r1f,
    r2f,
    r3f,
    r4f,
    ap,
    r1p,
    r2p,
    r3p,
    r4p,
    gsend,
    grecv,
    ssem,
    rsem,
    gssem,
    grsem,
    wssem,
    wrsem,
    lsem,
    fsem,
    osem,
):
    att = tokv
    gb = cotv
    g = lax.axis_index("dp")
    t = lax.axis_index("tensor")
    top, low = g // dp_low, g % dp_low
    mine = [(top // (1 << b)) % 2 for b in range(BITS)]

    def peer(b):
        return ((top + (1 - 2 * mine[b]) * (1 << b)) * dp_low + low, t)

    d0, d1 = peer(0)[0], peer(1)[0]
    core = (g, 1 - t)
    first = (jnp.where(t == 0, d0, d1), t)
    third = (jnp.where(t == 0, d1, d0), t)
    partners = (core, first, peer(2), third, peer(3))

    def place(b):
        rel = [mine[i] if (b >> i) & 1 == 0 else 1 - mine[i] for i in range(BITS)]
        one = rel[0] * 8 + rel[1] * 2
        two = rel[1] * 8 + rel[0] * 2
        return one + t * (two - one) + rel[2] * 4 + rel[3]

    places = [place(b) for b in range(16)]

    barrier = pltpu.get_barrier_semaphore()
    for partner in partners:
        pl.semaphore_signal(barrier, inc=1, device_id=partner, device_id_type=MESH)

    loads = [
        pltpu.make_async_copy(tok, tokv, lsem.at[0]),
        pltpu.make_async_copy(cot, cotv, lsem.at[1]),
        pltpu.make_async_copy(wqkv, wq.at[0], lsem.at[2]),
        pltpu.make_async_copy(wout, wo.at[pl.ds(0, 384)], lsem.at[3]),
    ]
    for c in loads:
        c.start()
    pl.semaphore_wait(barrier, len(partners))

    def weight_copy(i, src, dst):
        return pltpu.make_async_remote_copy(
            src_ref=src,
            dst_ref=dst,
            send_sem=wssem.at[i],
            recv_sem=wrsem.at[i],
            device_id=core,
            device_id_type=MESH,
        )

    weights = [
        weight_copy(0, wqkv, wq.at[1]),
        weight_copy(1, wout, wo.at[pl.ds(384, 384)]),
        weight_copy(2, wup, wup_x),
        weight_copy(3, wdn, wdn_x),
    ]
    for c in weights:
        c.start()

    def chunk_refs(c, is_ff):
        if is_ff:
            return 2 * FW, af.at[c], (r1f.at[c], r2f.at[c], r3f.at[c], r4f.at[c])
        return 384, ap.at[c - FF_CHUNKS], tuple(r.at[c - FF_CHUNKS] for r in (r1p, r2p, r3p, r4p))

    def rs_copy(stage, c, is_ff):
        width, a, rs = chunk_refs(c, is_ff)
        if stage == 0:
            slot = lax.rem(c, 2)
            src = sbuf.at[slot, :, :, pl.ds(0, width)]
            dst = r0.at[slot, :, :, pl.ds(0, width)]
        else:
            half = 16 >> stage
            src, dst = a.at[pl.ds(half, half)], rs[stage - 1]
        return pltpu.make_async_remote_copy(
            src_ref=src,
            dst_ref=dst,
            send_sem=ssem.at[c, stage],
            recv_sem=rsem.at[c, stage],
            device_id=partners[stage],
            device_id_type=MESH,
        )

    def finish(c, is_ff, total):
        if is_ff:
            cols = pl.ds(pl.multiple_of(c * FW, FW), FW)
            up_out[:, cols] = total[:, :FW]
            dn_out[:, cols] = total[:, FW:]
        elif c == FF_CHUNKS:
            pr_out[...] = total
        else:
            m = c - FF_CHUNKS - 1
            for part in range(3):
                qk_out[part, :, 128 * m : 128 * m + 128] = total[:, 128 * part : 128 * part + 128]

    def advance(stage, c, is_ff):
        width, a, rs = chunk_refs(c, is_ff)
        rs_copy(stage, c, is_ff).wait()
        if stage == 0:
            slot = lax.rem(c, 2)
            for pos in range(16):
                a[pos] = a[pos] + r0[slot, swap(pos), :, 0:width]
        elif stage < 4:
            half = 16 >> stage
            for pos in range(half):
                a[pos] = a[pos] + rs[stage - 1][pos]
        else:
            finish(c, is_ff, a[0].astype(f32) + rs[3][0].astype(f32))
        if stage < 4:
            rs_copy(stage + 1, c, is_ff).start()

    def event(e):
        for stage in range(4, -1, -1):
            c = e - stage - 1
            if 0 <= c < CHUNKS:
                advance(stage, c, c < FF_CHUNKS)
        if e < CHUNKS:
            rs_copy(0, e, e < FF_CHUNKS).start()

    s = slot_ref[0]
    loads[0].wait()
    loads[1].wait()
    zero_rows = jnp.zeros((PADDED - LENGTH, 128), bf16)
    for pp in range(PAIRS):
        for ref in (q, k, v, do):
            ref[pp, LENGTH:, :] = zero_rows
    nlg[LENGTH:, :] = zero_rows
    dlt[LENGTH:, :] = zero_rows

    def rows_of(i):
        return pl.ds(pl.multiple_of(i * 256, 256), 256)

    def permute(i, _):
        rows = rows_of(i)
        r = iota((256, 1), 0) + i * 256
        source = jnp.where(
            r < IMAGES * PATCHES,
            r + jnp.where(r >= PATCHES * s, PADDING, 0),
            PATCHES * s + r - IMAGES * PATCHES,
        )
        pick = (iota((256, LENGTH), 1) == source).astype(f32).astype(bf16)
        cp[rows] = dot(pick, cotv[...]).astype(bf16)
        x = dot(pick, tokv[...])
        xp[rows] = x.astype(bf16)
        standard, _unused = norm_rows(x)
        ni[rows] = (standard * ln1[...]).astype(bf16)
        return 0

    lax.fori_loop(0, 4, permute, 0)

    block = (iota((256, 256), 0) // HD == iota((256, 256), 1) // HD).astype(f32) * (1.0 / HD)
    block = block.astype(bf16)
    qg, kg = qgain[...], kgain[...]

    def head_norm(y, gain, pair_of, out, inv_out, factor):
        high, rest = split(y)
        centred = y - (dot(high, block) + dot(rest, block))
        inverse = lax.rsqrt(dot((centred * centred).astype(bf16), block) + EPS)
        standard = centred * inverse
        for half in range(2):
            lanes = slice(128 * half, 128 * half + 128)
            dest, inv_dest, dest_gain, pp = pair_of(half)
            dest[pp, 0:LENGTH, :] = (standard[:, lanes] * dest_gain).astype(bf16)
            inv_dest[pp] = inverse[:, lanes].astype(bf16)

    def project(p):
        for tile in range(3):
            parts = []
            for half in range(2):
                idx = 2 * tile + half
                part, m = idx // 3, idx % 3
                parts.append(wq[p, part, :, 128 * m : 128 * m + 128])
            y = dot(ni[...], jnp.concatenate(parts, axis=1))

            def pair_of(half, tile=tile):
                idx = 2 * tile + half
                pp = p * 3 + idx % 3
                if idx < 3:
                    return q, invq, qg * 0.125, pp
                return k, invk, kg, pp

            head_norm(y, None, pair_of, None, None, None)
        y = dot(ni[...], wq[p, 2]).astype(bf16)
        for m in range(3):
            v[p * 3 + m, 0:LENGTH, :] = y[:, 128 * m : 128 * m + 128]

    loads[2].wait()
    project(0)
    weights[0].wait()
    project(1)

    def low_lanes(rows):
        return iota((rows, 128), 1) < HD

    def two_heads(x, rows):
        low = low_lanes(rows)
        zero = jnp.zeros_like(x)
        return jnp.concatenate([jnp.where(low, x, zero), jnp.where(low, zero, x)], axis=0)

    def attend(pp, _):
        cols = pl.ds(pl.multiple_of(pp * 128, 128), 128)
        for start, rows, begin, end in WINDOWS:
            window = slice(start, start + rows)
            krows = 256 if rows > 48 else 48
            kwin = slice(start, start + krows)
            scores = dot_nt(two_heads(q[pp, window, :], rows), k[pp, kwin, :])
            weight = jnp.exp(scores).astype(bf16)
            kr = iota((krows, 256), 0) + start
            vone = jnp.concatenate([v[pp, kwin, :], jnp.ones((krows, 128), bf16)], axis=1)
            vone = jnp.where((kr >= begin) & (kr < end), vone, jnp.zeros_like(vone))
            both = dot(weight, vone)
            total = both[:, 128:]
            heads = both[:, :128] / total
            merged = jnp.where(low_lanes(rows), heads[:rows], heads[rows:]).astype(bf16)
            keep = iota((rows, 128), 0) + start < begin
            att[window, cols] = jnp.where(keep, att[window, cols], merged)
            lane = iota((rows, 128), 1) // 2
            sums = lse[window, :]
            sums = jnp.where((lane == 2 * pp) & ~keep, total[:rows], sums)
            sums = jnp.where((lane == 2 * pp + 1) & ~keep, total[rows:], sums)
            lse[window, :] = sums
        return 0

    lse[...] = jnp.ones_like(lse)
    lax.fori_loop(0, PAIRS, attend, 0)
    even = iota((LENGTH, 128), 1) % 2 == 0
    high, rest = split(-jnp.log(lse[...]))
    nlg[0:LENGTH, :] = jnp.where(even, high, rest)

    loads[3].wait()
    weights[1].wait()
    nm = big.at[:, pl.ds(1024, D)]
    act = big.at[:, pl.ds(0, 2 * FW)]
    gh = big.at[:, pl.ds(512, 2 * FW)]

    def middle(i, _):
        rows = rows_of(i)
        m = xp[rows].astype(f32) + dot(att[rows], wo[...])
        mid[rows] = m
        standard, _unused = norm_rows(m)
        nm[rows] = (standard * ln2[...]).astype(bf16)
        return 0

    lax.fori_loop(0, 4, middle, 0)

    def ff_loads(j, slot):
        cols = pl.ds(pl.multiple_of(j * FW, FW), FW)
        return [
            pltpu.make_async_copy(wup.at[:, cols], wus.at[slot, :, pl.ds(0, FW)], fsem.at[slot, 0]),
            pltpu.make_async_copy(
                wup_x.at[:, cols], wus.at[slot, :, pl.ds(FW, FW)], fsem.at[slot, 1]
            ),
            pltpu.make_async_copy(wdn.at[cols], wds.at[slot, pl.ds(0, FW)], fsem.at[slot, 2]),
            pltpu.make_async_copy(wdn_x.at[cols], wds.at[slot, pl.ds(FW, FW)], fsem.at[slot, 3]),
        ]

    weights[2].wait()
    weights[3].wait()
    for c in ff_loads(0, 0):
        c.start()
    outa[...] = jnp.zeros_like(outa)
    gna[...] = jnp.zeros_like(gna)

    def feed(j, _):
        slot = lax.rem(j, 2)
        for c in ff_loads(j, slot):
            c.wait()

        @pl.when(j < FF_CHUNKS - 1)
        def _():
            for c in ff_loads(j + 1, 1 - slot):
                c.start()

        wu, wd = wus[slot], wds[slot]
        for r in range(0, LENGTH, 256):
            rows = slice(r, r + 256)
            a, slope = gelu_and_slope(dot(nm[rows], wu))
            act[rows] = a.astype(bf16)
            gh[rows] = (dot_nt(cp[rows], wd) * slope).astype(bf16)
        outa[...] += dot(act[...], wd)
        gna[...] += dot_nt(gh[...], wu)
        up = dot_tn(nm[...], gh[...]).astype(bf16)
        dn = dot_tn(cp[...], act[...]).astype(bf16)
        for b in range(16):
            part = slice(48 * b, 48 * b + 48)
            af[j, places[b], :, 0:FW] = up[part, :FW]
            af[j, places[b], :, FW : 2 * FW] = dn[part, :FW]
            sbuf[slot, places[b], :, 0:FW] = up[part, FW:]
            sbuf[slot, places[b], :, FW : 2 * FW] = dn[part, FW:]
        for stage in range(4, -1, -1):

            @pl.when(j >= stage + 1)
            def _(stage=stage):
                advance(stage, j - stage - 1, True)

        rs_copy(0, j, True).start()
        return 0

    lax.fori_loop(0, FF_CHUNKS, feed, 0)

    def norm2_back(i, total):
        rows = rows_of(i)
        m = mid[rows]
        mid[rows] = m + outa[rows]
        standard, inverse = norm_rows(m)
        grad = gna[rows]
        grad_mid = cp[rows].astype(f32) + norm_rows_back(grad, standard, inverse, ln2[...])
        gna[rows] = grad_mid
        gb[rows] = grad_mid.astype(bf16)
        return total + jnp.sum(grad * standard, axis=0, keepdims=True)

    ln2_terms = lax.fori_loop(0, 4, norm2_back, jnp.zeros((1, D), f32))

    def put(c, slot, own, other):
        for b in range(16):
            part = slice(48 * b, 48 * b + 48)
            ap[c - FF_CHUNKS, places[b]] = own[part]
            sbuf[slot, places[b], :, 0:384] = other[part]

    pg = dot_tn(gb[...], att[...]).astype(bf16)
    put(FF_CHUNKS, 0, pg[:, :384], pg[:, 384:])
    event(FF_CHUNKS)

    ga = dot_nt(gb[...], wo[...])
    gab = ga.astype(bf16)
    for pp in range(PAIRS):
        do[pp, 0:LENGTH, :] = gab[:, 128 * pp : 128 * pp + 128]
    high, rest = split(gab.astype(f32) * att[...].astype(f32))
    gather = (iota((D, 128), 0) // HD == iota((D, 128), 1) // 2).astype(f32).astype(bf16)
    delta = dot(high, gather) + dot(rest, gather)
    high, rest = split(delta)
    dlt[0:LENGTH, :] = jnp.where(even, high, rest)

    block2 = (iota((256, 128), 0) % 128 // HD == iota((256, 128), 1) // HD).astype(f32) * (1.0 / HD)
    block2 = block2.astype(bf16)

    def head_mean(x):
        return dot(jnp.concatenate(split(x), axis=1), block2)

    def head_norm_back(grad, standard, inverse, gain):
        c = grad * gain
        return inverse * (c - head_mean(c) - standard * head_mean(c * standard))

    dq, dk, dv = (outa.at[:, pl.ds(128 * i, 128)] for i in range(3))

    def attend_back(pp, col):
        for start, rows, begin, end in WINDOWS:
            window = slice(start, start + rows)
            qrows = 256 if rows > 48 else 48
            qwin = slice(start, start + qrows)
            lane = iota((2 * rows, 128), 1)
            head = 2 * pp + jnp.where(iota((2 * rows, 128), 0) < rows, 0, 1)
            hot = (lane // 2 == head).astype(f32).astype(bf16)
            kb = k[pp, window, :]
            qb = q[pp, qwin, :]
            st = dot_nt(
                jnp.concatenate([two_heads(kb, rows), hot], axis=1),
                jnp.concatenate([qb, nlg[qwin, :]], axis=1),
            )
            pt = jnp.exp(st)
            qr = iota((qrows, 128), 0) + start
            valid = (qr >= begin) & (qr < end)
            dob = do[pp, qwin, :]
            zero = jnp.zeros_like(dob)
            dob = jnp.where(valid, dob, zero)
            dpt = dot_nt(
                jnp.concatenate([two_heads(v[pp, window, :], rows), -hot], axis=1),
                jnp.concatenate([dob, jnp.where(valid, dlt[qwin, :], zero)], axis=1),
            )
            dst = (pt * dpt).astype(bf16)
            dv2 = dot(pt.astype(bf16), dob)
            dk2 = dot(dst, qb)
            kr = iota((rows, 128), 0) + start
            kz = jnp.where((kr >= begin) & (kr < end), kb, jnp.zeros_like(kb))
            dq2 = dot_tn(dst, two_heads(kz, rows))[:rows]
            keep = kr < begin
            low = low_lanes(rows)
            dv[window, :] = jnp.where(keep, dv[window, :], jnp.where(low, dv2[:rows], dv2[rows:]))
            dk[window, :] = jnp.where(keep, dk[window, :], jnp.where(low, dk2[:rows], dk2[rows:]))
            dq[window, :] = jnp.where(keep, dq[window, :], dq2)
        standard = q[pp, 0:LENGTH, :].astype(f32) * (8.0 / qg)
        grad = dq[...] * 0.125
        q_terms = jnp.sum(grad * standard, axis=0, keepdims=True)
        big[:, col(0)] = head_norm_back(grad, standard, invq[pp].astype(f32), qg).astype(bf16)
        standard = k[pp, 0:LENGTH, :].astype(f32) * (1.0 / kg)
        grad = dk[...]
        k_terms = jnp.sum(grad * standard, axis=0, keepdims=True)
        big[:, col(1)] = head_norm_back(grad, standard, invk[pp].astype(f32), kg).astype(bf16)
        big[:, col(2)] = dv[...].astype(bf16)
        return q_terms, k_terms

    q_terms = jnp.zeros((1, 128), f32)
    k_terms = jnp.zeros((1, 128), f32)
    for m in range(3):

        def pair(i, carry, m=m):
            def col(part):
                return pl.ds(pl.multiple_of(768 * m + 384 * i + 128 * part, 128), 128)

            a, b = attend_back(3 * i + m, col)
            return carry[0] + a, carry[1] + b

        q_terms, k_terms = lax.fori_loop(0, 2, pair, (q_terms, k_terms))
        c = FF_CHUNKS + 1 + m
        both = dot_tn(ni[...], big[:, 768 * m : 768 * m + 768]).astype(bf16)
        put(c, c % 2, both[:, :384], both[:, 384:])
        event(c)

    def unpick(i):
        r = iota((256, 1), 0) + i * 256
        source = jnp.where(
            r < PATCHES * s,
            r,
            jnp.where(r < PATCHES * s + PADDING, r - PATCHES * s + IMAGES * PATCHES, r - PADDING),
        )
        return (iota((256, LENGTH), 1) == source).astype(f32).astype(bf16)

    def weight_of(m):
        return jnp.concatenate(
            [wq[p, part, :, 128 * m : 128 * m + 128] for p in range(2) for part in range(3)], axis=1
        )

    gsum = outa
    gsum[...] = dot_nt(big[:, 0:768], weight_of(0))
    gsum[...] += dot_nt(big[:, 768:1536], weight_of(1))
    event(CHUNKS)
    gsum[...] += dot_nt(big[:, 1536:2304], weight_of(2))
    igb = ni
    lob = cp

    def norm1_back(i, total):
        rows = rows_of(i)
        standard, inverse = norm_rows(xp[rows].astype(f32))
        grad = gsum[rows]
        igb[rows] = (gna[rows] + norm_rows_back(grad, standard, inverse, ln1[...])).astype(bf16)
        lob[rows] = mid[rows].astype(bf16)
        return total + jnp.sum(grad * standard, axis=0, keepdims=True)

    ln1_terms = lax.fori_loop(0, 4, norm1_back, jnp.zeros((1, D), f32))
    event(CHUNKS + 1)

    gsend[...] = jnp.zeros_like(gsend)
    for i in range(6):
        gsend[0, i : i + 1, :] = ln1_terms[:, 128 * i : 128 * i + 128]
        gsend[0, 6 + i : 7 + i, :] = ln2_terms[:, 128 * i : 128 * i + 128]
    gsend[0, 12:13, :] = q_terms
    gsend[0, 13:14, :] = k_terms

    def gain_copy(i):
        return pltpu.make_async_remote_copy(
            src_ref=gsend.at[i],
            dst_ref=grecv.at[i],
            send_sem=gssem.at[i],
            recv_sem=grsem.at[i],
            device_id=partners[i],
            device_id_type=MESH,
        )

    def gain_step(i):
        gain_copy(i).wait()
        total = gsend[i] + grecv[i]
        if i < 4:
            gsend[i + 1] = total
            gain_copy(i + 1).start()
        else:
            gains_out[...] = total

    gain_copy(0).start()

    def unpermute(i, _):
        rows = rows_of(i)
        pick = unpick(i)
        tokv[rows] = dot(pick, lob[...]).astype(bf16)
        cotv[rows] = dot(pick, igb[...]).astype(bf16)
        return 0

    lax.fori_loop(0, 4, unpermute, 0)
    outs = [
        pltpu.make_async_copy(tokv, lay_out, osem.at[0]),
        pltpu.make_async_copy(cotv, inp_out, osem.at[1]),
    ]
    for c in outs:
        c.start()
    gain_step(0)
    event(CHUNKS + 2)
    gain_step(1)
    gain_step(2)
    event(CHUNKS + 3)
    gain_step(3)
    gain_step(4)
    event(CHUNKS + 4)
    for c in outs:
        c.wait()


def local(
    tokens, segment, ln1_gain, w_qkv, q_gain, k_gain, w_out, ln2_gain, w_up, w_down, cotangent
):
    groups = lax.axis_size("dp")
    dp_low = groups // (1 << BITS)
    rows = D >> BITS
    own = lax.dynamic_slice_in_dim(segment, lax.axis_index("tensor") * LENGTH, LENGTH, 0)
    firsts = own[:: PATCHES][: IMAGES + 1]
    slot = jnp.sum(jnp.where(firsts == -1, jnp.arange(IMAGES + 1, dtype=jnp.int32), 0))
    hbm = pl.BlockSpec(memory_space=pl.ANY)
    vmem = pl.BlockSpec(memory_space=pltpu.VMEM)
    shape = jax.ShapeDtypeStruct
    half_ff = w_up.shape[1]
    ff, wide, n_proj = FF_CHUNKS, 2 * FW, CHUNKS - FF_CHUNKS

    def mem(*dims, dtype=bf16):
        return pltpu.VMEM(dims, dtype)

    outs = pl.pallas_call(
        functools.partial(kernel, dp_low),
        out_shape=(
            shape((LENGTH, D), bf16),
            shape((LENGTH, D), bf16),
            shape((rows, half_ff), f32),
            shape((rows, half_ff), f32),
            shape((rows, 384), f32),
            shape((3, rows, 384), f32),
            shape((16, 128), f32),
            shape((D, half_ff), bf16),
            shape((half_ff, D), bf16),
        ),
        in_specs=[pl.BlockSpec(memory_space=pltpu.SMEM), hbm, hbm, vmem, vmem, vmem, vmem]
        + [hbm] * 4,
        out_specs=(hbm, hbm, vmem, vmem, vmem, vmem, vmem, hbm, hbm),
        scratch_shapes=[
            mem(LENGTH, D),
            mem(LENGTH, D),
            mem(LENGTH, D),
            mem(LENGTH, D),
            mem(LENGTH, D),
            mem(PAIRS, PADDED, 128),
            mem(PAIRS, PADDED, 128),
            mem(PAIRS, PADDED, 128),
            mem(PAIRS, LENGTH, 128),
            mem(PAIRS, LENGTH, 128),
            mem(LENGTH, 128, dtype=f32),
            mem(PADDED, 128),
            mem(PADDED, 128),
            mem(LENGTH, D, dtype=f32),
            mem(LENGTH, D, dtype=f32),
            mem(LENGTH, D, dtype=f32),
            mem(LENGTH, 3 * D),
            mem(2, D, wide),
            mem(2, wide, D),
            mem(2, 3, D, 384),
            mem(D, D),
            mem(PAIRS, PADDED, 128),
            mem(2, 16, rows, wide),
            mem(2, 16, rows, wide),
            mem(ff, 16, rows, wide),
            mem(ff, 8, rows, wide),
            mem(ff, 4, rows, wide),
            mem(ff, 2, rows, wide),
            mem(ff, 1, rows, wide),
            mem(n_proj, 16, rows, 384),
            mem(n_proj, 8, rows, 384),
            mem(n_proj, 4, rows, 384),
            mem(n_proj, 2, rows, 384),
            mem(n_proj, 1, rows, 384),
            mem(5, 16, 128, dtype=f32),
            mem(5, 16, 128, dtype=f32),
            pltpu.SemaphoreType.DMA((CHUNKS, 5)),
            pltpu.SemaphoreType.DMA((CHUNKS, 5)),
            pltpu.SemaphoreType.DMA((5,)),
            pltpu.SemaphoreType.DMA((5,)),
            pltpu.SemaphoreType.DMA((4,)),
            pltpu.SemaphoreType.DMA((4,)),
            pltpu.SemaphoreType.DMA((4,)),
            pltpu.SemaphoreType.DMA((2, 4)),
            pltpu.SemaphoreType.DMA((2,)),
        ],
        compiler_params=pltpu.CompilerParams(
            collective_id=0, has_side_effects=True, vmem_limit_bytes=63 * 2**20
        ),
        name="layer",
    )(
        slot.reshape(1),
        tokens,
        cotangent,
        ln1_gain.reshape(1, D),
        ln2_gain.reshape(1, D),
        jnp.tile(q_gain, 2).reshape(1, 128),
        jnp.tile(k_gain, 2).reshape(1, 128),
        jnp.transpose(w_qkv, (1, 0, 2)),
        w_out,
        w_up,
        w_down,
    )
    layer_out, input_grad, up_grad, down_grad, proj_grad, qkv_grad, gains = outs[:7]
    if dp_low > 1:
        peers = [[hi * dp_low + lo for lo in range(dp_low)] for hi in range(1 << BITS)]

        def rest(x, axis):
            return lax.psum_scatter(
                x, "dp", scatter_dimension=axis, axis_index_groups=peers, tiled=True
            )

        up_grad, down_grad, proj_grad = rest(up_grad, 0), rest(down_grad, 0), rest(proj_grad, 0)
        qkv_grad = rest(qkv_grad, 1)
        gains = lax.psum(gains, "dp", axis_index_groups=peers)
    q_terms, k_terms = gains[12], gains[13]
    return (
        layer_out,
        input_grad,
        gains[0:6].reshape(D),
        jnp.transpose(qkv_grad, (1, 0, 2)),
        q_terms[:HD] + q_terms[HD:],
        k_terms[:HD] + k_terms[HD:],
        proj_grad.T,
        gains[6:12].reshape(D),
        up_grad,
        down_grad.T,
    )


def solution(mesh):
    return jax.shard_map(
        local,
        mesh=mesh,
        in_specs=(
            P(("dp", "tensor"), None),
            P("dp"),
            P(),
            P(None, None, "tensor"),
            P(),
            P(),
            P("tensor", None),
            P(),
            P(None, "tensor"),
            P("tensor", None),
            P(("dp", "tensor"), None),
        ),
        out_specs=(
            P(("dp", "tensor"), None),
            P(("dp", "tensor"), None),
            P(),
            P("dp", None, "tensor"),
            P(),
            P(),
            P("tensor", "dp"),
            P(),
            P("dp", "tensor"),
            P("tensor", "dp"),
        ),
        check_vma=False,
    )
```

time: 1160 us -> 153 us (0.13)
  waiting for transfers between devices: 570 us -> 0 us
  matrix products: 276 us -> 0 us
  other arithmetic: 170 us -> 2.04 us
  Pallas kernels: 0 us -> 136 us
  local copies, waits for them, and re-layouts: 68.6 us -> 13.8 us
  blocking collectives: 41.4 us -> 0 us
  between operations: 14.7 us -> 0.68 us
    reduce_scatter x9 -> x0, waiting for transfers between devices: 523 us -> none  [the longest x1 141 us: local(): lax.psum_scatter(weight_grads[2], 'dp', scatter_dimension=0, tiled=True)]
    dot_general x49 -> x0, matrix products: 276 us -> none  [the longest x11 86 us: contract(): lax.dot_general(left, right, (((left_axis,), (right_axis,)), ((), ())), p...]
    pallas_call x0 -> x1, Pallas kernels: none -> 136 us  [local(): pl.pallas_call(functools.partial(kernel, dp_low), out_shape=(shape((LENGT...]
    sub x4 -> x0, other arithmetic: 68.2 us -> none  [one_block(): exponent = jnp.exp(scores - row_top)]
    convert_element_type x11 -> x0, other arithmetic: 49.8 us -> none  [the longest x4 27.9 us: one_block(): grad_scores = (attn_probs * (grad_probs - centre)).astype(jnp.bfloat16)]
    all_gather x5 -> x0, waiting for transfers between devices: 47.1 us -> none  [the longest x2 26.2 us: gather_middle(): return lax.all_gather(values, 'tensor', axis=0, tiled=True)]
    reduce_sum x14 -> x1, other arithmetic: 45.5 us -> 0.64 us  [local(): jnp.sum(jnp.where(firsts == -1, jnp.arange(IMAGES + 1, dtype=jnp.int32), 0))]
    psum x1 -> x0, blocking collectives: 41.4 us -> none  [local(): lax.psum((gain_terms[0], gain_terms[1], gain_terms[2], gain_terms[3]), ('...]
  transfers between devices with their start and end apart: 14 -> 0, of which waited for: 12 -> 0; matrix products, arithmetic and copies ran while one was open for 10% -> 0% of each run, Pallas kernels for 0% -> 0%
where the time goes in v1:
time: 153 us
  Pallas kernels  136 us (89%)
  local copies, waits for them, and re-layouts  13.8 us (9%)
  other arithmetic  2.04 us (1%)
    pallas_call x1, Pallas kernels, local(): pl.pallas_call(functools.partial(kernel, dp_low), out_shape=(shape((LENGT...  136 us
    unnamed x16, local copies, waits for them, and re-layouts  6.68 us

profile of v1, /device:TPU:0, one launch (start us, length us, event | category | flops | bytes accessed | tf_op | source)
XLA Modules:
  0.0 152.6 jit_solution(10177252735061005386)
XLA Ops:
  0.6 0.7 tile.4
  1.3 0.6 reshape_tile.6.qgain
  1.9 0.7 tile.5
  2.6 0.6 reshape_tile.7.kgain
  3.1 1.3 reshape.44.ln1
  4.4 1.3 reshape.45.ln2
  5.7 0.7 dynamic_slice.3
  6.4 0.1 slice.31
  6.5 0.6 fusion
  7.1 136.1 %layer.1 = (bf16[1024,768]{1,0:T(8,128)(2,1)}, bf16[1024,768]{1,0:T(8,128)(2,1)}, f32[48,1536]{1,0:T(8,128)}, f32[48,1536]{1,0:T(8,128)}, f32[48,384]{1,0:T(8,12...) custom-call(s32[1]{0:T(128)} %bitcast.slot_ref, ...), custom_call_target="tpu_custom_call" | custom-call | tf_op jit(solution)/shard_map/layer/pallas_call | solution.py:666
  143.2 1.4 add_bitcast_fusion
  144.6 1.4 slice_bitcast_fusion
  145.9 2.8 %copy.27 = bf16[1024,768]{1,0:T(8,128)(2,1)} copy(bf16[1024,768]{1,0:T(8,128)(2,1)} %get-tuple-element.38) | data formatting | bytes 3145728
  148.7 0.0 copy-done
  148.7 0.0 copy-start.1
  148.7 1.1 copy.28
  149.9 0.0 copy-done.3
  149.9 0.7 copy.29
  150.6 0.0 copy-done.4
  150.6 0.6 copy.30
  151.2 0.0 copy-done.2
  151.2 0.7 copy.31
  151.9 0.0 copy-done.1
  151.9 0.7 copy.32
  (4 shorter events, 0.0 us)
Async XLA Ops:
  145.9 2.8 %copy-start = (bf16[1024,768]{1,0:T(8,128)(2,1)S(1)}, bf16[1024,768]{1,0:T(8,128)(2,1)}, u32[]{:S(2)}) copy-start(bf16[1024,768]{1,0:T(8,128)(2,1)} %get-tuple-element.39) | copy-start | bytes 4718596
  148.7 1.2 copy-start.3
  148.7 1.9 %copy-start.4 = (f32[48,384]{1,0:T(8,128)S(1)}, f32[48,384]{1,0:T(8,128)}, u32[]{:S(2)}) copy-start(f32[48,384]{1,0:T(8,128)} %get-tuple-element.21) | copy-start | bytes 221188
  148.7 2.5 %copy-start.2 = (f32[48,1536]{1,0:T(8,128)S(1)}, f32[48,1536]{1,0:T(8,128)}, u32[]{:S(2)}) copy-start(f32[48,1536]{1,0:T(8,128)} %get-tuple-element.46) | copy-start | bytes 884740
  148.7 3.2 %copy-start.1 = (f32[48,1536]{1,0:T(8,128)S(1)}, f32[48,1536]{1,0:T(8,128)}, u32[]{:S(2)}) copy-start(f32[48,1536]{1,0:T(8,128)} %get-tuple-element.23) | copy-start | bytes 884740
